TPU v7x, 512 devices: a whole 4x4x16 slice. The times are simulated.
512 devices in a mesh: dp: 32 (over x, y, core), tensor: 16 (over z).
Axes of the slice: x: 4, y: 4, z: 16, core: 2. Of those that a mesh axis runs over, the one named last changes fastest.
Arguments:
- tokens: bfloat16 [2048, 14848], P('dp', 'tensor'), may hold values from -6 to 6
- base_up_matrix: bfloat16 [14848, 32, 928], P('tensor', 'dp'), may hold values from -0.046875 to 0.046875
- adapter_down_maps: bfloat16 [64, 64, 14848], P('dp', None, 'tensor'), may hold values from -0.046875 to 0.046875
- adapter_up_maps: bfloat16 [64, 64, 29696], P('dp', None, 'tensor'), may hold values from -0.75 to 0.75
- request_adapter: int32 [2048, 1], P('dp'), may hold values from 0 to 63; in each aligned block of 64 rows (0 to 63, 64 to 127, ...) at most 2 rows name the same one
- adapter_storage: int32 [64], replicated, may hold values from 0 to 63, each once
Outputs:
- hidden: bfloat16 [2048, 29696], P('dp', 'tensor')
Inputs may be any that keep to these rules, and one draw needn't show every extreme that they name: `request_adapter`: within the 64 rows of one dp index no adapter is named more than 2 times, a bound that some block reaches; every adapter is named somewhere. `adapter_storage`: A permutation of the slots.
All inputs are finite; a program needn't handle non-finite values.
Results may differ from a plain program's by a relative error of at most 0.025.
Values may be sent and summed in bfloat16 or wider, within the bound.
A program may use at most 64 MiB of HBM per device.

v0:
```python
import jax
import jax.numpy as jnp
from jax import lax
from jax.sharding import PartitionSpec as P


def route_positions(row_ids, adapter_storage):
    count = adapter_storage.shape[0]
    onehot = row_ids[:, None] == jnp.arange(count, dtype=jnp.int32)[None, :]
    slot_index = jnp.sum(jnp.where(onehot, adapter_storage[None, :], 0), axis=1)
    before = jnp.cumsum(onehot.astype(jnp.int32), axis=0) - 1
    row_rank = jnp.sum(jnp.where(onehot, before, 0), axis=1)
    return (slot_index, row_rank)


def local(
    tokens, base_up_matrix, adapter_down_maps, adapter_up_maps, request_adapter, adapter_storage
):
    groups = lax.axis_size("dp")
    shards = lax.axis_size("tensor")
    tok_rows = tokens.shape[0]
    width_part = tokens.shape[1]
    block_width = base_up_matrix.shape[2]
    share_width = block_width // shards
    local_adapters = adapter_down_maps.shape[0]
    capacity = max(2, 2 * tok_rows // (groups * local_adapters))
    slots_total = groups * local_adapters * capacity
    w_local = base_up_matrix.reshape(width_part, block_width)
    output_width = adapter_up_maps.shape[2]
    own_slot, own_rank = route_positions(request_adapter[:, 0], adapter_storage)
    own_position = own_slot * capacity + own_rank
    partial_value = jnp.dot(
        lax.all_gather(tokens, "dp", axis=0, tiled=True),
        w_local,
        preferred_element_type=jnp.float32,
    ).astype(jnp.bfloat16)
    buffer = jnp.zeros((slots_total, width_part), jnp.bfloat16).at[own_position].set(tokens)
    buffer = buffer.reshape(groups, local_adapters, capacity, width_part)
    shrink_part = jnp.einsum(
        "nakd,ard->nakr",
        lax.all_to_all(buffer, "dp", split_axis=0, concat_axis=0, tiled=True),
        adapter_down_maps,
        preferred_element_type=jnp.float32,
    )
    reduced_state = lax.psum(shrink_part.astype(jnp.bfloat16), "tensor")
    grown = jnp.einsum(
        "dbxl,blp->dbxp", reduced_state, adapter_up_maps, preferred_element_type=jnp.float32
    ).astype(jnp.bfloat16)
    returned = lax.all_to_all(grown, "dp", split_axis=0, concat_axis=0, tiled=True)
    delta_rows = returned.reshape(slots_total, output_width)[own_position]
    swapped = lax.all_to_all(partial_value, "dp", split_axis=0, concat_axis=1, tiled=True)
    swapped = swapped.reshape(tok_rows, groups, shards, share_width)
    summed = lax.psum_scatter(swapped, "tensor", scatter_dimension=2, tiled=True).astype(
        jnp.float32
    )
    summed = summed.reshape(tok_rows, output_width)
    return jax.nn.gelu(summed + delta_rows.astype(jnp.float32), approximate=False).astype(
        jnp.bfloat16
    )


def solution(mesh):
    return jax.shard_map(
        local,
        mesh=mesh,
        in_specs=(
            P("dp", "tensor"),
            P("tensor", "dp", None),
            P("dp", None, "tensor"),
            P("dp", None, "tensor"),
            P("dp", None),
            P(),
        ),
        out_specs=P("dp", "tensor"),
        check_vma=False,
    )
```

profile of v0, /device:TPU:1, one launch (start us, length us, event | category | flops | bytes accessed | tf_op | source)
XLA Modules:
  0.0 270.5 jit_solution(115803822633272640)
XLA Ops:
  6.5 0.7 all-gather.2.cloned.1.call-update
  7.3 70.3 %all-gather.2.cloned.1.call-done = bf16[2048,928]{1,0:T(8,128)(2,1)} async-done(((bf16[64,928]{1,0:T(8,128)(2,1)}), bf16[2048,928]{1,0:T(8,128)(2,1)}) %all-gather.2.cloned.1.call-update) | async-done | bytes 3801104 | tf_op jit(solution)/shard_map/all_gather | solution.py:33
  77.6 8.2 %convolution_convert_fusion = bf16[2048,928]{0,1:T(8,128)(2,1)} fusion(bf16[2048,928]{1,0:T(8,128)(2,1)} %all-gather.2.cloned.1.call-done, bf16[928,1,928]{2,0,1:T(8,128)(2,1)S(1)} %copy-done), kind=kOutput, calls=%fused_computation.2 | convolution fusion | flops 3529310208 | bytes 9324544 | tf_op jit(solution)/shard_map/dot_general | solution.py:32
  85.8 6.3 %copy.15 = bf16[2048,928]{1,0:T(8,128)(2,1)} copy(bf16[2048,928]{0,1:T(8,128)(2,1)} %convolution_convert_fusion) | data formatting | bytes 7602176 | tf_op jit(solution)/shard_map/convert_element_type | solution.py:36
  92.1 56.0 %all_to_all.26 = bf16[32,64,928]{2,1,0:T(8,128)(2,1)} all-to-all(bf16[32,64,928]{2,1,0:T(8,128)(2,1)} %bitcast.33), channel_id=1, replica_groups=mesh['dp'=32,'tensor'=16] {'dp'}, dimensions={0} | all-to-all | bytes 7602176 | tf_op jit(solution)/shard_map/all_to_all | solution.py:51
  148.1 12.6 %copy.25 = bf16[64,32,928]{0,1,2:T(8,128)(2,1)} copy(bf16[64,32,928]{2,0,1:T(8,128)(2,1)} %bitcast.32) | data formatting | bytes 7602176 | tf_op jit(solution)/shard_map/reshape | solution.py:52
  160.8 0.6 copy-done.3
  161.4 0.1 reduce_window_sum.11
  161.5 0.2 select_reduce_fusion.1
  161.7 1.3 scatter_custom_fusion
  163.1 0.1 reshape.53
  163.2 12.7 %all_to_all.27 = bf16[32,2,2,928]{3,2,1,0:T(2,128)(2,1)S(1)} all-to-all(bf16[32,2,2,928]{3,2,1,0:T(2,128)(2,1)S(1)} %reshape.53), channel_id=1, replica_groups=mesh['dp'=32,'tensor'=16] {'dp'}, dimensions={0} | all-to-all | bytes 475136 | tf_op jit(solution)/shard_map/all_to_all | solution.py:41
  175.9 0.2 fusion.2
  176.2 51.8 %psum.7 = bf16[32,2,2,64]{3,0,2,1:T(8,128)(2,1)S(1)} all-reduce(bf16[32,2,2,64]{3,0,2,1:T(8,128)(2,1)S(1)} %fusion.2), channel_id=1, replica_groups=mesh['dp'=32,'tensor'=16] {'tensor'}, use_global_device_ids=true, to_apply=%region_5.6 | all-reduce | flops 8192 | bytes 32768 | tf_op jit(solution)/shard_map/psum | solution.py:45
  228.0 0.3 fusion
  228.3 1.2 copy.20
  229.4 11.4 %all-to-all-start.2 = ((bf16[32,2,2,1856]{3,2,1,0:T(2,128)(2,1)}), bf16[32,2,2,1856]{3,2,1,0:T(2,128)(2,1)S(1)}, u32[]{:S(2)}, u32[]{:S(2)}) async-start(bf16[32,2,2,1856]{3,2,1,0:T(2,128)(2,1)} %copy.20), calls=%async_computation.3 | async-start | bytes 983040 | tf_op jit(solution)/shard_map/all_to_all | solution.py:49
  240.9 11.4 %all-to-all-done.2 = bf16[32,2,2,1856]{3,2,1,0:T(2,128)(2,1)S(1)} async-done(((bf16[32,2,2,1856]{3,2,1,0:T(2,128)(2,1)}), bf16[32,2,2,1856]{3,2,1,0:T(2,128)(2,1)S(1)}, u32[]{:S(2)}, u32[]{:S(2)}) %all-to-all-start.2) | async-done | bytes 475168 | tf_op jit(solution)/shard_map/all_to_all | solution.py:49
  252.3 0.4 reshape.54
  252.6 1.4 gather_fusion
  254.1 4.2 %reduce-scatter.2.cloned.1.call-done = bf16[64,32,1,58]{0,1,3,2:T(8,128)(2,1)} async-done(((bf16[64,32,16,58]{0,1,3,2:T(8,128)(2,1)}), bf16[64,32,1,58]{0,1,3,2:T(8,128)(2,1)}) %reduce-scatter.2.cloned.1.call-update) | async-done | bytes 237584 | tf_op jit(solution)/shard_map/reduce_scatter | solution.py:53
  258.3 2.0 copy.18
  260.3 0.6 reshape.56
  260.9 2.7 %fusion.5 = bf16[64,1856]{1,0:T(8,128)(2,1)} fusion(f32[64,1856]{1,0:T(8,128)S(1)} %reshape.56, bf16[64,1856]{1,0:T(8,128)(2,1)} %gather_fusion), kind=kLoop, calls=%fused_computation.11 | loop fusion | flops 7958528 | bytes 950272 | tf_op jit(solution)/shard_map/convert_element_type | solution.py:57
  (15 shorter events, 0.2 us)
Async XLA Ops:
  6.5 71.1 %copy-start = (bf16[928,1,928]{2,0,1:T(8,128)(2,1)S(1)}, bf16[928,1,928]{2,0,1:T(8,128)(2,1)}, u32[]{:S(2)}) copy-start(bf16[928,1,928]{2,0,1:T(8,128)(2,1)} %param.7) | copy-start | bytes 5167108
  6.5 71.1 %all-gather.2.cloned.1.call-start = ((), (), s32[]{:S(2)}) async-start(), calls=%async_computation.4 | async-start | bytes 4325376 | tf_op jit(solution)/shard_map/all_gather | solution.py:33
  7.3 251.0 %reduce-scatter.2.cloned.1.call-start = ((), (), s32[]{:S(2)}) async-start(), calls=%async_computation.5 | async-start | bytes 8077312 | tf_op jit(solution)/shard_map/reduce_scatter | solution.py:53
  160.7 0.7 copy-start.3
  160.7 0.8 copy-start.4
  160.7 15.2 %copy-start.2 = (bf16[2,64,928]{2,1,0:T(8,128)(2,1)S(1)}, bf16[2,64,928]{2,1,0:T(8,128)(2,1)}, u32[]{:S(2)}) copy-start(bf16[2,64,928]{2,1,0:T(8,128)(2,1)} %param.8) | copy-start | bytes 712708
  160.7 67.3 %copy-start.1 = (bf16[2,64,1856]{2,1,0:T(8,128)(2,1)S(1)}, bf16[2,64,1856]{2,1,0:T(8,128)(2,1)}, u32[]{:S(2)}) copy-start(bf16[2,64,1856]{2,1,0:T(8,128)(2,1)} %param.9) | copy-start | bytes 1425412
  229.4 22.8 %all-to-all-start.2 = ((bf16[32,2,2,1856]{3,2,1,0:T(2,128)(2,1)}), bf16[32,2,2,1856]{3,2,1,0:T(2,128)(2,1)S(1)}, u32[]{:S(2)}, u32[]{:S(2)}) async-start(bf16[32,2,2,1856]{3,2,1,0:T(2,128)(2,1)} %copy.20), calls=%async_computation.3 | async-start | bytes 983040 | tf_op jit(solution)/shard_map/all_to_all | solution.py:49
Sparse Core Ops, SparseCore 0:
  10.5 67.0 all-gather.1
  160.9 97.3 reduce-scatter.1
where the time goes:
time: 271 us; the launch traced here: 270 us
  blocking collectives  121 us (45%)
  waiting for transfers between devices  86.7 us (32%)
  local copies, waits for them, and re-layouts  26.5 us (10%)
  between operations  13.5 us (5%)
  starting transfers between devices  11.5 us (4%)
  matrix products  8.69 us (3%)
  other arithmetic  3.08 us (1%)
    all_gather x1, waiting for transfers between devices, local(): lax.all_gather(tokens, 'dp', axis=0, tiled=True)  70.3 us
    all_to_all x1, blocking collectives, local(): lax.all_to_all(partial_value, 'dp', split_axis=0, concat_axis=1, tiled=True)  56 us
    psum x1, blocking collectives, local(): reduced_state = lax.psum(shrink_part.astype(jnp.bfloat16), 'tensor')  51.8 us
    all_to_all x1, blocking collectives, local(): lax.all_to_all(buffer, 'dp', split_axis=0, concat_axis=0, tiled=True)  12.7 us
    reshape x1, local copies, waits for them, and re-layouts, local(): swapped = swapped.reshape(tok_rows, groups, shards, share_width)  12.6 us
    all_to_all x1, starting transfers between devices, local(): lax.all_to_all(grown, 'dp', split_axis=0, concat_axis=0, tiled=True)  11.4 us
    all_to_all x1, waiting for transfers between devices, local(): lax.all_to_all(grown, 'dp', split_axis=0, concat_axis=0, tiled=True)  11.4 us
    dot_general x1, matrix products, local(): jnp.dot(lax.all_gather(tokens, 'dp', axis=0, tiled=True), w_local, prefer...  8.18 us
  transfers between devices with their start and end apart: 3, of which 3 were waited for; matrix products, arithmetic and copies ran while one was open for 2% of the time, Pallas kernels for 0%

commit v1 on v0

v1 whole, which is shorter than its diff:
```python
import jax
import jax.numpy as jnp
from jax import lax
from jax.experimental import pallas as pl
from jax.experimental.pallas import tpu as pltpu
from jax.sharding import PartitionSpec as P

MESH = pl.DeviceIdType.MESH
F32 = jnp.float32
BF16 = jnp.bfloat16

NZ = 16
NDP = 32
ROWS = 64
WIDTH = 928
WPAD = 1024
SHARE = 58
SPAD = 64
CHUNKS = 4
CTOK = 512
LAG = 2
COLS = 1856
CPAD = 1920

OFFSETS = (
    ((0, 0), (1, 0), (3, 0), (0, 1)),
    ((0, 3), (1, 1), (3, 3), (2, 0)),
    ((0, 2), (1, 3), (3, 1), (2, 1)),
    ((1, 2), (3, 2), (2, 3), (2, 2)),
)


def digits(values):
    return sum(v << (2 * i) for i, v in enumerate(values))


def pick(values, n):
    if isinstance(n, int):
        return values[n]
    return lax.rem(lax.shift_right_logical(jnp.int32(digits(values)), 2 * n), 4)


def offset(n, q):
    return pick([OFFSETS[m][q][0] for m in range(CHUNKS)], n), pick([OFFSETS[m][q][1] for m in range(CHUNKS)], n)


def dot_nt(a, b):
    return lax.dot_general(a, b, (((1,), (1,)), ((), ())), preferred_element_type=F32)


def dot_nn(a, b):
    return lax.dot_general(a, b, (((1,), (0,)), ((), ())), preferred_element_type=F32)


def iota(shape, dim):
    return lax.broadcasted_iota(jnp.int32, shape, dim)


def erf(x):
    x = jnp.clip(x, -4.0, 4.0)
    s = x * x
    p = -2.72614225801306e-10
    for c in (
        2.77068142495902e-08,
        -2.10102402082508e-06,
        -5.69250639462346e-05,
        -7.34990630326855e-04,
        -2.95459980854025e-03,
        -1.60960333262415e-02,
    ):
        p = p * s + c
    q = -1.45660718464996e-05
    for c in (-2.13374055278905e-04, -1.68282697438203e-03, -7.37332916720468e-03, -1.42647390514189e-02):
        q = q * s + c
    return x * p / q


def kernel(
    tok_ref, w_ref, down_ref, up_ref, req_ref, sto_ref, out_ref,
    xbuf, wt, y, h, lbuf, sbuf, total, rbuf, stack, sel,
    zsend, zrecv, zred, zgather, shr, shrx, dbuf, ebuf, fbuf, gbuf,
    ag_s, ag_r, fw_s, fw_r, l_s, l_r, s_s, s_r, r_s, r_r,
    z1_s, z1_r, z2_s, z2_r, e_s, e_r, g_s, g_r,
):
    dp = lax.axis_index("dp")
    z = lax.axis_index("tensor")
    core = lax.rem(dp, 2)
    cy = lax.rem(dp // 2, 4)
    cx = dp // 8
    yc = cy * 2 + core

    def dev(x, yy, c):
        return (lax.rem(x, 4) * 4 + lax.rem(yy, 4)) * 2 + c

    partner = dev(cx, cy, 1 - core)

    def remote(src, dst, ssem, rsem, target):
        return pltpu.make_async_remote_copy(
            src_ref=src, dst_ref=dst, send_sem=ssem, recv_sem=rsem, device_id=target, device_id_type=MESH
        )

    barrier = pltpu.get_barrier_semaphore()

    @pl.loop(1, NDP)
    def _(i):
        pl.semaphore_signal(barrier, inc=1, device_id=(lax.rem(dp + i, NDP), z), device_id_type=MESH)

    @pl.loop(1, NZ)
    def _(i):
        pl.semaphore_signal(barrier, inc=1, device_id=(dp, lax.rem(z + i, NZ)), device_id_type=MESH)

    onehot = req_ref[...] == iota((ROWS, 64), 1)
    slot = jnp.sum(jnp.where(onehot, sto_ref[...], 0), axis=1, keepdims=True)
    lower = (iota((ROWS, ROWS), 1) < iota((ROWS, ROWS), 0)).astype(F32).astype(BF16)
    before = dot_nn(lower, onehot.astype(F32).astype(BF16))
    rank = jnp.sum(jnp.where(onehot, before, 0.0), axis=1, keepdims=True)
    place = slot.astype(F32) * 2.0 + rank
    xbuf[0, core] = jnp.broadcast_to(place, (ROWS, WPAD)).astype(BF16)
    xbuf[0, core, :, 0:WIDTH] = tok_ref[...]

    pl.semaphore_wait(barrier, NDP - 1 + NZ - 1)

    def forward(n, q):
        p = 4 * n + q
        return remote(xbuf.at[p, core], xbuf.at[p, core], fw_s.at[p], fw_r.at[p], (partner, z))

    def gather(n, q):
        p = 4 * n + q
        dx, dy = offset(n, q)
        return remote(
            xbuf.at[0, core], xbuf.at[p, core], ag_s.at[p], ag_r.at[p], (dev(cx + dx, cy + dy, core), z)
        )

    forward(0, 0).start()
    for n in range(CHUNKS):
        for q in range(4):
            if (n, q) != (0, 0):
                gather(n, q).start()

    wt[...] = jnp.zeros_like(wt)

    @pl.loop(0, 4)
    def _(b):
        row = iota((256, WIDTH), 0)
        unit = (b * 4 + row // SPAD) * SHARE + row % SPAD
        pickrow = jnp.where((row % SPAD < SHARE) & (unit == iota((256, WIDTH), 1)), 1.0, 0.0).astype(BF16)
        wt[b, :, 0:WIDTH] = dot_nt(pickrow, w_ref[...]).astype(BF16)

    wt[4, 0:128, 0:WIDTH] = down_ref[...]
    dbuf[...] = jnp.zeros_like(dbuf)

    def relay(n):
        for q in range(4):

            @pl.when(n * 4 + q > 0)
            def _():
                gather(n, q).wait_recv()
                forward(n, q).start()

    def multiply(n):
        for q in range(4):
            p = 4 * n + q
            remote(xbuf.at[p, 1 - core], xbuf.at[p, 1 - core], fw_s.at[p], fw_r.at[p], (partner, z)).wait_recv()

        @pl.loop(0, 4)
        def _(b):
            x = xbuf[pl.ds(4 * n, 4)].reshape(CTOK, WPAD)
            y[n, pl.ds(4 * b, 4)] = dot_nt(wt[b], x).reshape(4, SPAD, CTOK).astype(BF16)

        x = xbuf[pl.ds(4 * n, 4)].reshape(CTOK, WPAD)
        low = dot_nt(wt[4, 0:128], x).astype(BF16)
        for q in range(4):
            h[4 * n + q] = low[:, q * 128 : (q + 1) * 128]

    def long_hop(n, s, src):
        way = 1 - 2 * lax.rem(n, 2)
        return remote(src, lbuf.at[n, s], l_s.at[n, s], l_r.at[n, s], (dp, lax.rem(z + way + NZ, NZ)))

    def short_hop(n, s, src):
        way = 1 - 2 * lax.rem(n, 2)
        return remote(src, sbuf.at[n, s], s_s.at[n, s], s_r.at[n, s], (dp, lax.rem(z - way + NZ, NZ)))

    def long_target(n, s):
        return lax.rem(z + (1 - 2 * lax.rem(n, 2)) * (8 - s) + NZ, NZ)

    def short_target(n, s):
        return lax.rem(z - (1 - 2 * lax.rem(n, 2)) * (7 - s) + NZ, NZ)

    def result(n, q, c):
        dx, dy = offset(n, q)
        target = dev(cx + 4 - dx, cy + 4 - dy, c)
        return remote(total.at[n, q], rbuf.at[dp], r_s.at[n, q, c], r_r.at[n, q, core], (target, z))

    def result_arrives(n, q, c):
        dx, dy = offset(n, q)
        source = dev(cx + dx, cy + dy, c)
        return remote(total.at[n, q], rbuf.at[source], r_s.at[n, q, c], r_r.at[n, q, c], (partner, z))

    def stage(n, s):
        @pl.when(s == 0)
        def _():
            multiply(n)
            long_hop(n, 0, y.at[n, long_target(n, 0)]).start()
            short_hop(n, 0, y.at[n, short_target(n, 0)]).start()

        @pl.when((s >= 1) & (s <= 7))
        def _():
            here = lbuf.at[n, s - 1]
            long_hop(n, s - 1, here).wait_recv()
            lbuf[n, s - 1] = (lbuf[n, s - 1].astype(F32) + y[n, long_target(n, s)].astype(F32)).astype(BF16)
            long_hop(n, s, here).start()

        @pl.when((s >= 1) & (s <= 6))
        def _():
            here = sbuf.at[n, s - 1]
            short_hop(n, s - 1, here).wait_recv()
            sbuf[n, s - 1] = (sbuf[n, s - 1].astype(F32) + y[n, short_target(n, s)].astype(F32)).astype(BF16)
            short_hop(n, s, here).start()

        @pl.when(s == 8)
        def _():
            short_hop(n, 6, sbuf.at[n, 6]).wait_recv()
            long_hop(n, 7, lbuf.at[n, 7]).wait_recv()
            both = lbuf[n, 7].astype(F32) + sbuf[n, 6].astype(F32) + y[n, z].astype(F32)
            both = both.astype(BF16)
            for q in range(4):
                total[n, q] = both[:, q * 128 : (q + 1) * 128]
            for q in range(4):
                for c in range(2):

                    @pl.when((n > 0) | (q > 0) | (core != c))
                    def _():
                        result(n, q, c).start()

            @pl.when(n == 0)
            def _():
                rbuf[dp] = total[0, 0]

    def tick(t):
        for n in range(CHUNKS):

            @pl.when(t == max(0, LAG * n - 1))
            def _():
                relay(n)

        @pl.loop(0, CHUNKS)
        def _(n):
            s = t - LAG * n

            @pl.when((s >= 0) & (s <= 8))
            def _():
                stage(n, s)

    lane64 = iota((64, 128), 1)

    def shrink():
        key = dp * 4

        @pl.loop(0, 16)
        def _(p):
            n, q = p // 4, p % 4
            dx = pick([OFFSETS[m][0][0] for m in range(4)], n)
            dy = pick([OFFSETS[m][0][1] for m in range(4)], n)
            for j in range(1, 4):
                ox, oy = offset(n, j)
                dx = jnp.where(q == j, ox, dx)
                dy = jnp.where(q == j, oy, dy)
            x = lax.rem(cx + 4 - dx, 4)
            yy = lax.rem(cy + 4 - dy, 4)
            meta = dot_nt(
                jnp.where(iota((16, 128), 1) == 127, 1.0, 0.0).astype(BF16),
                xbuf[p, :, :, WPAD - 128 : WPAD].reshape(128, 128),
            )[0:1]
            row = iota((128, 128), 0)
            home = (yy * 2 + iota((128, 128), 1) // 64) * 4 + x
            wanted = key + 2 * (row // 64) + row % 2
            hit = ((row % 64) // 2 == home) & (meta.astype(jnp.int32) == wanted)
            sel[p] = jnp.where(hit, 1.0, 0.0).astype(BF16)

        acc = jnp.zeros((128, 128), F32)
        for p in range(16):
            acc = acc + dot_nt(sel[p], h[p])
        part = jnp.where(lane64 < 64, acc[0:64], acc[64:128])
        for i in range(NZ):
            zsend[i] = part[4 * i : 4 * i + 4]

        @pl.loop(1, NZ)
        def _(i):
            other = lax.rem(z + i, NZ)
            remote(zsend.at[other], zrecv.at[z], z1_s.at[i], z1_r.at[i], (dp, other)).start()

        zrecv[z] = zsend[z]

    def reduce():
        @pl.loop(1, NZ)
        def _(i):
            other = lax.rem(z + NZ - i, NZ)
            remote(zsend.at[other], zrecv.at[other], z1_s.at[i], z1_r.at[i], (dp, other)).wait_recv()

        whole = zrecv[0]
        for i in range(1, NZ):
            whole = whole + zrecv[i]
        zred[...] = whole

        @pl.loop(1, NZ)
        def _(i):
            other = lax.rem(z + i, NZ)
            remote(zred, zgather.at[z], z2_s.at[i], z2_r.at[i], (dp, other)).start()

        zgather[z] = zred[...]

    def grow():
        @pl.loop(1, NZ)
        def _(i):
            other = lax.rem(z + NZ - i, NZ)
            remote(zred, zgather.at[other], z2_s.at[i], z2_r.at[i], (dp, other)).wait_recv()

        for i in range(NZ):
            shr[4 * i : 4 * i + 4] = zgather[i]
        rows = shr[...]
        for g in range(8):
            eight = rows[8 * g : 8 * g + 8]
            lane = lane64[0:8]
            shrx[16 * g : 16 * g + 8] = jnp.where(lane < 64, eight, 0.0)
            shrx[16 * g + 8 : 16 * g + 16] = jnp.where(lane < 64, 0.0, eight)
        grown = dot_nn(shrx[...].astype(BF16), up_ref[...])
        dbuf[:, :, 0:COLS] = grown.reshape(8, 16, COLS).astype(BF16)

        @pl.loop(1, 8)
        def _(i):
            other = lax.rem(yc + i, 8)
            target = dev(cx, other // 2, lax.rem(other, 2))
            remote(dbuf.at[other], ebuf.at[yc], e_s.at[i], e_r.at[i], (target, z)).start()

        ebuf[yc] = dbuf[yc]

    def sort():
        @pl.loop(1, 8)
        def _(i):
            other = lax.rem(yc + 8 - i, 8)
            target = dev(cx, other // 2, lax.rem(other, 2))
            remote(dbuf.at[other], ebuf.at[other], e_s.at[i], e_r.at[i], (target, z)).wait_recv()

        to = iota((128, 128), 0)
        source = ((to // 4) % 8) * 16 + ((to // 2) % 2) * 8 + (to // 32) * 2 + to % 2
        perm = jnp.where(iota((128, 128), 1) == source, 1.0, 0.0).astype(BF16)
        fbuf[...] = dot_nn(perm, ebuf[...].reshape(128, CPAD)).reshape(4, 32, CPAD).astype(BF16)

        @pl.loop(1, 4)
        def _(i):
            other = lax.rem(cx + i, 4)
            remote(fbuf.at[other], gbuf.at[cx], g_s.at[i], g_r.at[i], (dev(other, cy, core), z)).start()

        gbuf[cx] = fbuf[cx]

    def deltas():
        @pl.loop(1, 4)
        def _(i):
            other = lax.rem(cx + 4 - i, 4)
            remote(fbuf.at[other], gbuf.at[other], g_s.at[i], g_r.at[i], (dev(other, cy, core), z)).wait_recv()

        mine = (place.astype(jnp.int32) == iota((ROWS, 128), 1)).astype(F32).astype(BF16)
        return dot_nn(mine, gbuf[...].reshape(128, CPAD))[:, 0:COLS]

    last = LAG * (CHUNKS - 1) + 8
    full = LAG * (CHUNKS - 1)

    steps = ((full + 1, shrink), (full + 3, reduce), (full + 5, grow), (full + 7, sort))
    done = 0
    for until, what in steps:

        @pl.loop(done, until)
        def _(t):
            tick(t)

        what()
        done = until

    @pl.loop(done, last + 1)
    def _(t):
        tick(t)

    delta = deltas()

    @pl.loop(0, CHUNKS)
    def _(n):
        for q in range(4):
            for c in range(2):

                @pl.when((n > 0) | (q > 0) | (core != c))
                def _():
                    result_arrives(n, q, c).wait_recv()

    for k in range(NDP):
        stack[k * SHARE : (k + 1) * SHARE] = rbuf[k].astype(F32)[0:SHARE]
    turn = jnp.where(iota((ROWS, 128), 1) == core * 64 + iota((ROWS, 128), 0), 1.0, 0.0).astype(BF16)
    base = dot_nt(turn, stack[...].astype(BF16))
    v = base + delta
    out_ref[...] = (0.5 * v * (1.0 + erf(v * 0.7071067811865476))).astype(BF16)

    @pl.loop(0, CHUNKS)
    def _(n):
        for q in range(4):
            forward(n, q).wait_send()

            @pl.when(n * 4 + q > 0)
            def _():
                gather(n, q).wait_send()

            for c in range(2):

                @pl.when((n > 0) | (q > 0) | (core != c))
                def _():
                    result(n, q, c).wait_send()

        @pl.loop(0, 8)
        def _(s):
            long_hop(n, s, lbuf.at[n, s]).wait_send()

        @pl.loop(0, 7)
        def _(s):
            short_hop(n, s, sbuf.at[n, s]).wait_send()

    @pl.loop(1, NZ)
    def _(i):
        other = lax.rem(z + i, NZ)
        remote(zsend.at[other], zrecv.at[z], z1_s.at[i], z1_r.at[i], (dp, other)).wait_send()
        remote(zred, zgather.at[z], z2_s.at[i], z2_r.at[i], (dp, other)).wait_send()

    @pl.loop(1, 8)
    def _(i):
        remote(dbuf.at[yc], ebuf.at[yc], e_s.at[i], e_r.at[i], (partner, z)).wait_send()

    @pl.loop(1, 4)
    def _(i):
        remote(fbuf.at[cx], gbuf.at[cx], g_s.at[i], g_r.at[i], (partner, z)).wait_send()


def local(tokens, base_up_matrix, adapter_down_maps, adapter_up_maps, request_adapter, adapter_storage):
    dma = pltpu.SemaphoreType.DMA
    vmem = pl.BlockSpec(memory_space=pltpu.VMEM)
    return pl.pallas_call(
        kernel,
        out_shape=jax.ShapeDtypeStruct((ROWS, COLS), BF16),
        in_specs=[vmem] * 6,
        out_specs=vmem,
        scratch_shapes=[
            pltpu.VMEM((16, 2, ROWS, WPAD), BF16),
            pltpu.VMEM((5, 256, WPAD), BF16),
            pltpu.VMEM((CHUNKS, NZ, SPAD, CTOK), BF16),
            pltpu.VMEM((16, 128, 128), BF16),
            pltpu.VMEM((CHUNKS, 8, SPAD, CTOK), BF16),
            pltpu.VMEM((CHUNKS, 7, SPAD, CTOK), BF16),
            pltpu.VMEM((CHUNKS, 4, SPAD, 128), BF16),
            pltpu.VMEM((NDP, SPAD, 128), BF16),
            pltpu.VMEM((COLS, 128), F32),
            pltpu.VMEM((16, 128, 128), BF16),
            pltpu.VMEM((NZ, 4, 128), F32),
            pltpu.VMEM((NZ, 4, 128), F32),
            pltpu.VMEM((4, 128), F32),
            pltpu.VMEM((NZ, 4, 128), F32),
            pltpu.VMEM((64, 128), F32),
            pltpu.VMEM((128, 128), F32),
            pltpu.VMEM((8, 16, CPAD), BF16),
            pltpu.VMEM((8, 16, CPAD), BF16),
            pltpu.VMEM((4, 32, CPAD), BF16),
            pltpu.VMEM((4, 32, CPAD), BF16),
            dma((16,)), dma((16,)), dma((16,)), dma((16,)),
            dma((CHUNKS, 8)), dma((CHUNKS, 8)), dma((CHUNKS, 7)), dma((CHUNKS, 7)),
            dma((CHUNKS, 4, 2)), dma((CHUNKS, 4, 2)),
            dma((NZ,)), dma((NZ,)), dma((NZ,)), dma((NZ,)),
            dma((8,)), dma((8,)), dma((4,)), dma((4,)),
        ],
        compiler_params=pltpu.CompilerParams(
            collective_id=0, has_side_effects=True, vmem_limit_bytes=56 * 1024 * 1024
        ),
        name="gather_sum_exchange",
    )(
        tokens,
        base_up_matrix.reshape(WIDTH, WIDTH),
        adapter_down_maps.reshape(128, WIDTH),
        adapter_up_maps.reshape(128, COLS),
        request_adapter,
        adapter_storage.reshape(1, 64),
    )


def solution(mesh):
    return jax.shard_map(
        local,
        mesh=mesh,
        in_specs=(
            P("dp", "tensor"),
            P("tensor", "dp", None),
            P("dp", None, "tensor"),
            P("dp", None, "tensor"),
            P("dp", None),
            P(),
        ),
        out_specs=P("dp", "tensor"),
        check_vma=False,
    )
```

time: 271 us -> 122 us (0.45)
  blocking collectives: 121 us -> 0 us
  Pallas kernels: 0 us -> 119 us
  waiting for transfers between devices: 86.7 us -> 0 us
  local copies, waits for them, and re-layouts: 26.5 us -> 3.01 us
  between operations: 13.5 us -> 0.01 us
  starting transfers between devices: 11.5 us -> 0 us
  matrix products: 8.69 us -> 0 us
  other arithmetic: 3.08 us -> 0 us
    pallas_call x0 -> x1, Pallas kernels: none -> 119 us  [local(): pl.pallas_call(kernel, out_shape=jax.ShapeDtypeStruct((ROWS, COLS), BF16)...]
    all_gather x1 -> x0, waiting for transfers between devices: 70.3 us -> none  [local(): lax.all_gather(tokens, 'dp', axis=0, tiled=True)]
    all_to_all x2 -> x0, blocking collectives: 68.7 us -> none  [the longest x1 56 us: local(): lax.all_to_all(partial_value, 'dp', split_axis=0, concat_axis=1, tiled=True)]
    psum x1 -> x0, blocking collectives: 51.8 us -> none  [local(): reduced_state = lax.psum(shrink_part.astype(jnp.bfloat16), 'tensor')]
    reshape x5 -> x0, local copies, waits for them, and re-layouts: 15.7 us -> none  [the longest x1 12.6 us: local(): swapped = swapped.reshape(tok_rows, groups, shards, share_width)]
    all_to_all x1 -> x0, starting transfers between devices: 11.4 us -> none  [local(): lax.all_to_all(grown, 'dp', split_axis=0, concat_axis=0, tiled=True)]
    all_to_all x1 -> x0, waiting for transfers between devices: 11.4 us -> none  [local(): lax.all_to_all(grown, 'dp', split_axis=0, concat_axis=0, tiled=True)]
    dot_general x3 -> x0, matrix products: 8.69 us -> none  [the longest x1 8.18 us: local(): jnp.dot(lax.all_gather(tokens, 'dp', axis=0, tiled=True), w_local, prefer...]
  transfers between devices with their start and end apart: 3 -> 0, of which waited for: 3 -> 0; matrix products, arithmetic and copies ran while one was open for 2% -> 0% of each run, Pallas kernels for 0% -> 0%
where the time goes in v1:
time: 122 us
  Pallas kernels  119 us (98%)
  local copies, waits for them, and re-layouts  3.01 us (2%)
    pallas_call x1, Pallas kernels, local(): pl.pallas_call(kernel, out_shape=jax.ShapeDtypeStruct((ROWS, COLS), BF16)...  119 us
    unnamed x2, local copies, waits for them, and re-layouts  3.01 us

profile of v1, /device:TPU:1, one launch (start us, length us, event | category | flops | bytes accessed | tf_op | source)
XLA Modules:
  0.0 121.6 jit_solution(14148318348338989234)
XLA Ops:
  0.0 1.4 %copy.7.req_ref = s32[64,1]{1,0:T(8,128)} copy(s32[64,1]{0,1:T(1,128)} %param.10) | data formatting | bytes 512 | tf_op args[4]
  1.4 118.6 %gather_sum_exchange.1 = bf16[64,1856]{1,0:T(8,128)(2,1)} custom-call(bf16[64,928]{1,0:T(8,128)(2,1)} %tok_ref.1, bf16[928,928]{1,0:T(8,128)(2,1)} %bitcast.4, bf16[128,928]{1,0:T(8,128)(2,1)} %bitcast.6, bf16[128,1856]{1,0:T(8,128)(2,1)} %bitcast.5, s32[64,1]{1,0:T(8,128)} %copy.7.req_ref, s32[1,64]{1,0:T(1,128)} %bitcast.7), custom_call_target="tpu_custom_call" | custom-call | tf_op jit(solution)/shard_map/gather_sum_exchange/pallas_call | solution.py:442
  119.9 1.7 %copy.9 = bf16[64,1856]{1,0:T(8,128)(2,1)} copy(bf16[64,1856]{1,0:T(8,128)(2,1)} %gather_sum_exchange.1) | data formatting | bytes 475136

commit v2 on v1

v2 whole, which is shorter than its diff:
```python
import jax
import jax.numpy as jnp
from jax import lax
from jax.experimental import pallas as pl
from jax.experimental.pallas import tpu as pltpu
from jax.sharding import PartitionSpec as P

MESH = pl.DeviceIdType.MESH
F32 = jnp.float32
BF16 = jnp.bfloat16

NZ = 16
NDP = 32
ROWS = 64
WIDTH = 928
WPAD = 1024
SHARE = 58
SPAD = 64
CHUNKS = 4
CTOK = 512
CROWS = 240
COLS = 1856
CPAD = 1920

OFFSETS = (
    ((0, 0), (1, 0), (3, 0), (0, 1)),
    ((0, 3), (1, 1), (1, 3), (3, 1)),
    ((3, 3), (2, 0), (0, 2), (2, 1)),
    ((2, 3), (1, 2), (3, 2), (2, 2)),
)
POS = {offset: 4 * n + q for n, chunk in enumerate(OFFSETS) for q, offset in enumerate(chunk)}

PARTS = tuple(
    [(1, 0, "F"), (3, 0, "F"), (2, 0, "a"), (2, 0, "b")]
    + [(f, g, part) for f in range(4) for g, part in ((1, "F"), (3, "F"), (2, "a"), (2, "b"))]
)

ORDER = (
    "w0", "w1", "w2", "w3", "10F", "30F", "01F", "03F", "20a", "m00",
    "13F", "s00", "11F", "20b", "m01", "m02", "m03", "31F", "33F", "02a",
    "02b", "l0", "s01", "12b", "12a", "m10", "s10", "m11", "21F", "23F",
    "m12", "32a", "32b", "m13", "s02", "m20", "s20", "22a", "22b", "s11",
    "m21", "m22", "m23", "m30", "s30", "s03", "m31", "m32", "s21", "m33",
    "l1", "s12", "l2", "l3", "shrink", "s31", "s22", "s13", "s32", "s23",
    "s14", "reduce", "s33", "s24", "s04", "s34", "s25", "s15", "grow", "s35",
    "s05", "s26", "s36", "s16", "s06", "sort", "s37", "s27", "s17", "s07",
    "s38", "s28", "delta", "s18", "s08",
)


def dot_nt(a, b):
    return lax.dot_general(a, b, (((1,), (1,)), ((), ())), preferred_element_type=F32)


def dot_nn(a, b):
    return lax.dot_general(a, b, (((1,), (0,)), ((), ())), preferred_element_type=F32)


def iota(shape, dim):
    return lax.broadcasted_iota(jnp.int32, shape, dim)


def erf(x):
    x = jnp.clip(x, -4.0, 4.0)
    s = x * x
    p = -2.72614225801306e-10
    for c in (
        2.77068142495902e-08,
        -2.10102402082508e-06,
        -5.69250639462346e-05,
        -7.34990630326855e-04,
        -2.95459980854025e-03,
        -1.60960333262415e-02,
    ):
        p = p * s + c
    q = -1.45660718464996e-05
    for c in (-2.13374055278905e-04, -1.68282697438203e-03, -7.37332916720468e-03, -1.42647390514189e-02):
        q = q * s + c
    return x * p / q


def kernel(
    tok_ref, w_any, down_any, up_any, req_ref, sto_ref, out_ref,
    w_ref, down_ref, up_ref, xbuf, wt, low, ylong, yshort, first, h, lbuf, sbuf, both, total, rbuf, stack, sel,
    zsend, zrecv, zred, zgather, shr, shrx, dbuf, ebuf, fbuf, gbuf, dterm,
    in_s, ag_s, ag_r, fw_s, fw_r, l_s, l_r, s_s, s_r, r_s, r_r,
    z1_s, z1_r, z2_s, z2_r, e_s, e_r, g_s, g_r,
):
    dp = lax.axis_index("dp")
    z = lax.axis_index("tensor")
    core = lax.rem(dp, 2)
    cy = lax.rem(dp // 2, 4)
    cx = dp // 8
    yc = cy * 2 + core
    way = 1 - 2 * core

    def dev(x, yy, c):
        return (lax.rem(x, 4) * 4 + lax.rem(yy, 4)) * 2 + c

    partner = dev(cx, cy, 1 - core)
    steps = {
        ("f", 1): dev(cx + core, cy + 1 - core, core),
        ("f", 3): dev(cx + 3 * core, cy + 3 * (1 - core), core),
        ("g", 1): dev(cx + 1 - core, cy + core, core),
        ("g", 3): dev(cx + 3 * (1 - core), cy + 3 * core, core),
    }

    def remote(src, dst, ssem, rsem, target):
        return pltpu.make_async_remote_copy(
            src_ref=src, dst_ref=dst, send_sem=ssem, recv_sem=rsem, device_id=target, device_id_type=MESH
        )

    barrier = pltpu.get_barrier_semaphore()

    @pl.loop(1, NZ)
    def _(i):
        pl.semaphore_signal(barrier, inc=1, device_id=(dp, lax.rem(z + i, NZ)), device_id_type=MESH)

    @pl.loop(1, NDP)
    def _(i):
        pl.semaphore_signal(barrier, inc=1, device_id=(lax.rem(dp + i, NDP), z), device_id_type=MESH)

    loads = {
        "w": pltpu.make_async_copy(w_any, w_ref, in_s.at[0]),
        "down": pltpu.make_async_copy(down_any, down_ref, in_s.at[1]),
        "up": pltpu.make_async_copy(up_any, up_ref, in_s.at[2]),
    }
    for load in loads.values():
        load.start()

    diagonal = iota((ROWS, ROWS), 0) == iota((ROWS, ROWS), 1)
    adapter = jnp.sum(jnp.where(diagonal, req_ref[...], 0), axis=1, keepdims=True)
    onehot = adapter == iota((ROWS, 64), 1)
    slot = jnp.sum(jnp.where(onehot, sto_ref[...], 0), axis=1, keepdims=True)
    lower = (iota((ROWS, ROWS), 1) < iota((ROWS, ROWS), 0)).astype(F32).astype(BF16)
    before = dot_nn(lower, onehot.astype(F32).astype(BF16))
    rank = jnp.sum(jnp.where(onehot, before, 0.0), axis=1, keepdims=True)
    place = slot.astype(F32) * 2.0 + rank
    xbuf[0, core, :, WPAD - 128 : WPAD] = jnp.broadcast_to(place, (ROWS, 128)).astype(BF16)
    xbuf[0, core, :, 0:WIDTH] = tok_ref[...]

    pl.semaphore_wait(barrier, NDP - 1 + NZ - 1)

    def where_at(f, g):
        return POS[g, f] + core * (POS[f, g] - POS[g, f])

    def part_copy(f, g, part):
        axis, d = ("f", f) if g == 0 else ("g", g)
        if part == "F":
            start, size, back, way_on = 0, ROWS, d, d
        else:
            start, size = (0, ROWS // 2) if part == "a" else (ROWS // 2, ROWS // 2)
            back = way_on = 1 if part == "a" else 3
        if part == "F":
            source = (0, 0) if g == 0 else (f, 0)
        else:
            source = (back, 0) if g == 0 else (f, back)
        i = PARTS.index((f, g, part))
        rows = pl.ds(start, size)
        return remote(
            xbuf.at[where_at(*source), core, rows], xbuf.at[where_at(f, g), core, rows],
            ag_s.at[i], ag_r.at[i], (steps[axis, way_on], z),
        )

    def forward(p):
        return remote(xbuf.at[p, core], xbuf.at[p, core], fw_s.at[p], fw_r.at[p], (partner, z))

    for part in ((1, 0, "F"), (3, 0, "F"), (0, 1, "F"), (0, 3, "F")):
        part_copy(*part).start()
    forward(0).start()

    low[...] = jnp.zeros_like(low)
    dbuf[...] = jnp.zeros_like(dbuf)
    ylong[:, :, CROWS - 8 : CROWS] = jnp.zeros((CHUNKS, 8, 8, 128), F32)
    yshort[:, :, CROWS - 8 : CROWS] = jnp.zeros((CHUNKS, 8, 8, 128), F32)

    arrived = {}

    def gathered(f, g, part):
        part_copy(f, g, part).wait_recv()
        if part == "F":
            half = "a" if (f if g == 0 else g) == 1 else "b"
            part_copy(2, 0, half).start() if g == 0 else part_copy(f, 2, half).start()
        else:
            arrived[f, g] = arrived.get((f, g), 0) + 1
            if arrived[f, g] < 2:
                return
        forward(where_at(f, g)).start()
        if g == 0:
            part_copy(f, 1, "F").start()
            part_copy(f, 3, "F").start()

    def offsets(b):
        return (8 - 2 * b, 9 + 2 * b, 7 - 2 * b, 10 + 2 * b)

    def weights(b):
        if b == 0:
            loads["w"].wait()
        row = iota((256, WIDTH), 0)
        plane = jnp.zeros((256, WIDTH), jnp.int32)
        for j, o in enumerate(offsets(b)):
            plane = jnp.where(row // SPAD == j, lax.rem(z + way * o + NZ, NZ), plane)
        unit = plane * SHARE + row % SPAD
        pickrow = jnp.where((row % SPAD < SHARE) & (unit == iota((256, WIDTH), 1)), 1.0, 0.0).astype(BF16)
        wt[b, :, WPAD - 128 : WPAD] = jnp.zeros((256, 128), BF16)
        wt[b, :, 0:WIDTH] = dot_nt(pickrow, w_ref[...]).astype(BF16)
        if b == 3:
            loads["down"].wait()
            low[:, 0:WIDTH] = down_ref[...]

    def multiply(n, b):
        if b == 0:
            for q in range(4):
                p = 4 * n + q
                remote(xbuf.at[p, 1 - core], xbuf.at[p, 1 - core], fw_s.at[p], fw_r.at[p], (partner, z)).wait_recv()
        x = xbuf[4 * n : 4 * n + 4].reshape(CTOK, WPAD)
        part = dot_nt(wt[b], x)
        for j in range(4):
            dest, s = (ylong, yshort)[j % 2], 2 * b + j // 2
            for q in range(4):
                dest[n, s, q * SHARE : (q + 1) * SHARE] = part[j * SPAD : j * SPAD + SHARE, q * 128 : (q + 1) * 128]

    def down(n):
        x = xbuf[4 * n : 4 * n + 4].reshape(CTOK, WPAD)
        part = dot_nt(low[...], x).astype(BF16)
        for q in range(4):
            h[4 * n + q] = part[:, q * 128 : (q + 1) * 128]

    def long_hop(n, s, src):
        return remote(src, lbuf.at[n, s], l_s.at[n, s], l_r.at[n, s], (dp, lax.rem(z + way + NZ, NZ)))

    def short_hop(n, s, src):
        return remote(src, sbuf.at[n, s], s_s.at[n, s], s_r.at[n, s], (dp, lax.rem(z - way + NZ, NZ)))

    def result(n, q, c):
        dx, dy = OFFSETS[n][q]
        target = dev(cx + 4 - dx, cy + 4 - dy, c)
        return remote(total.at[n, q], rbuf.at[dp], r_s.at[n, q, c], r_r.at[n, q, core], (target, z))

    def result_arrives(n, q, c):
        dx, dy = OFFSETS[n][q]
        source = dev(cx + dx, cy + dy, c)
        return remote(total.at[n, q], rbuf.at[source], r_s.at[n, q, c], r_r.at[n, q, c], (partner, z))

    def others(n, q, c, what):
        if n == 0 and q == 0:

            @pl.when(core != c)
            def _():
                what(n, q, c)

        else:
            what(n, q, c)

    def stage(n, s):
        if s == 0:
            first[n, 0] = ylong[n, 0].astype(BF16)
            long_hop(n, 0, first.at[n, 0]).start()
            first[n, 1] = yshort[n, 0].astype(BF16)
            short_hop(n, 0, first.at[n, 1]).start()
        if 1 <= s <= 7:
            here = lbuf.at[n, s - 1]
            long_hop(n, s - 1, here).wait_recv()
            lbuf[n, s - 1] = (lbuf[n, s - 1].astype(F32) + ylong[n, s]).astype(BF16)
            long_hop(n, s, here).start()
        if 1 <= s <= 6:
            here = sbuf.at[n, s - 1]
            short_hop(n, s - 1, here).wait_recv()
            sbuf[n, s - 1] = (sbuf[n, s - 1].astype(F32) + yshort[n, s]).astype(BF16)
            short_hop(n, s, here).start()
        if s == 8:
            short_hop(n, 6, sbuf.at[n, 6]).wait_recv()
            long_hop(n, 7, lbuf.at[n, 7]).wait_recv()
            both[...] = lbuf[n, 7].astype(F32) + sbuf[n, 6].astype(F32) + yshort[n, 7]
            for q in range(4):
                total[n, q] = both[q * SHARE : q * SHARE + SPAD].astype(BF16)
                for c in range(2):
                    others(n, q, c, lambda *a: result(*a).start())
            if n == 0:
                rbuf[dp] = total[0, 0]

    lane64 = iota((64, 128), 1)

    def shrink():
        key = dp * 4
        for n in range(CHUNKS):
            for q in range(4):
                p = 4 * n + q
                dx, dy = OFFSETS[n][q]
                x = lax.rem(cx + 4 - dx, 4)
                yy = lax.rem(cy + 4 - dy, 4)
                meta = dot_nt(
                    jnp.where(iota((16, 128), 1) == 127, 1.0, 0.0).astype(BF16),
                    xbuf[p, :, :, WPAD - 128 : WPAD].reshape(128, 128),
                )[0:1]
                row = iota((128, 128), 0)
                home = (yy * 2 + iota((128, 128), 1) // 64) * 4 + x
                wanted = key + 2 * (row // 64) + row % 2
                hit = ((row % 64) // 2 == home) & (meta.astype(jnp.int32) == wanted)
                sel[p] = jnp.where(hit, 1.0, 0.0).astype(BF16)
        acc = jnp.zeros((128, 128), F32)
        for p in range(16):
            acc = acc + dot_nt(sel[p], h[p])
        part = jnp.where(lane64 < 64, acc[0:64], acc[64:128])
        for i in range(NZ):
            zsend[i] = part[4 * i : 4 * i + 4]

        @pl.loop(1, NZ)
        def _(i):
            other = lax.rem(z + i, NZ)
            remote(zsend.at[other], zrecv.at[z], z1_s.at[i], z1_r.at[i], (dp, other)).start()

        zrecv[z] = zsend[z]

    def reduce():
        @pl.loop(1, NZ)
        def _(i):
            other = lax.rem(z + NZ - i, NZ)
            remote(zsend.at[other], zrecv.at[other], z1_s.at[i], z1_r.at[i], (dp, other)).wait_recv()

        whole = zrecv[0]
        for i in range(1, NZ):
            whole = whole + zrecv[i]
        zred[...] = whole

        @pl.loop(1, NZ)
        def _(i):
            other = lax.rem(z + i, NZ)
            remote(zred, zgather.at[z], z2_s.at[i], z2_r.at[i], (dp, other)).start()

        zgather[z] = zred[...]

    def grow():
        @pl.loop(1, NZ)
        def _(i):
            other = lax.rem(z + NZ - i, NZ)
            remote(zred, zgather.at[other], z2_s.at[i], z2_r.at[i], (dp, other)).wait_recv()

        for i in range(NZ):
            shr[4 * i : 4 * i + 4] = zgather[i]
        rows = shr[...]
        for g in range(8):
            eight = rows[8 * g : 8 * g + 8]
            lane = lane64[0:8]
            shrx[16 * g : 16 * g + 8] = jnp.where(lane < 64, eight, 0.0)
            shrx[16 * g + 8 : 16 * g + 16] = jnp.where(lane < 64, 0.0, eight)
        loads["up"].wait()
        grown = dot_nn(shrx[...].astype(BF16), up_ref[...])
        dbuf[:, :, 0:COLS] = grown.reshape(8, 16, COLS).astype(BF16)

        @pl.loop(1, 8)
        def _(i):
            other = lax.rem(yc + i, 8)
            target = dev(cx, other // 2, lax.rem(other, 2))
            remote(dbuf.at[other], ebuf.at[yc], e_s.at[i], e_r.at[i], (target, z)).start()

        ebuf[yc] = dbuf[yc]

    def sort():
        @pl.loop(1, 8)
        def _(i):
            other = lax.rem(yc + 8 - i, 8)
            target = dev(cx, other // 2, lax.rem(other, 2))
            remote(dbuf.at[other], ebuf.at[other], e_s.at[i], e_r.at[i], (target, z)).wait_recv()

        to = iota((128, 128), 0)
        source = ((to // 4) % 8) * 16 + ((to // 2) % 2) * 8 + (to // 32) * 2 + to % 2
        perm = jnp.where(iota((128, 128), 1) == source, 1.0, 0.0).astype(BF16)
        fbuf[...] = dot_nn(perm, ebuf[...].reshape(128, CPAD)).reshape(4, 32, CPAD).astype(BF16)

        @pl.loop(1, 4)
        def _(i):
            other = lax.rem(cx + i, 4)
            remote(fbuf.at[other], gbuf.at[cx], g_s.at[i], g_r.at[i], (dev(other, cy, core), z)).start()

        gbuf[cx] = fbuf[cx]

    def deltas():
        @pl.loop(1, 4)
        def _(i):
            other = lax.rem(cx + 4 - i, 4)
            remote(fbuf.at[other], gbuf.at[other], g_s.at[i], g_r.at[i], (dev(other, cy, core), z)).wait_recv()

        mine = (place.astype(jnp.int32) == iota((ROWS, 128), 1)).astype(F32).astype(BF16)
        dterm[...] = dot_nn(mine, gbuf[...].reshape(128, CPAD))[:, 0:COLS]

    adapters = {"shrink": shrink, "reduce": reduce, "grow": grow, "sort": sort, "delta": deltas}
    for word in ORDER:
        if word in adapters:
            adapters[word]()
        elif word[0] == "w":
            weights(int(word[1]))
        elif word[0] == "m":
            multiply(int(word[1]), int(word[2]))
        elif word[0] == "s":
            stage(int(word[1]), int(word[2]))
        elif word[0] == "l":
            down(int(word[1]))
        else:
            gathered(int(word[0]), int(word[1]), word[2])

    for part in PARTS:
        if part != (0, 0, "F"):
            part_copy(*part).wait_send()
    for p in range(16):
        forward(p).wait_send()
    for n in range(CHUNKS):
        for s in range(8):
            long_hop(n, s, lbuf.at[n, s]).wait_send()
        for s in range(7):
            short_hop(n, s, sbuf.at[n, s]).wait_send()

    @pl.loop(1, NZ)
    def _(i):
        other = lax.rem(z + i, NZ)
        remote(zsend.at[other], zrecv.at[z], z1_s.at[i], z1_r.at[i], (dp, other)).wait_send()
        remote(zred, zgather.at[z], z2_s.at[i], z2_r.at[i], (dp, other)).wait_send()

    @pl.loop(1, 8)
    def _(i):
        remote(dbuf.at[yc], ebuf.at[yc], e_s.at[i], e_r.at[i], (partner, z)).wait_send()

    @pl.loop(1, 4)
    def _(i):
        remote(fbuf.at[cx], gbuf.at[cx], g_s.at[i], g_r.at[i], (partner, z)).wait_send()

    for n in range(CHUNKS):
        for q in range(4):
            for c in range(2):
                others(n, q, c, lambda *a: result(*a).wait_send())
    for n in range(CHUNKS):
        for q in range(4):
            for c in range(2):
                others(n, q, c, lambda *a: result_arrives(*a).wait_recv())

    for k in range(NDP):
        stack[k * SHARE : (k + 1) * SHARE] = rbuf[k].astype(F32)[0:SHARE]
    turn = jnp.where(iota((ROWS, 128), 1) == core * 64 + iota((ROWS, 128), 0), 1.0, 0.0).astype(BF16)
    v = dot_nt(turn, stack[...].astype(BF16)) + dterm[...]
    out_ref[...] = (0.5 * v * (1.0 + erf(v * 0.7071067811865476))).astype(BF16)


def local(tokens, base_up_matrix, adapter_down_maps, adapter_up_maps, request_adapter, adapter_storage):
    dma = pltpu.SemaphoreType.DMA
    vmem = pl.BlockSpec(memory_space=pltpu.VMEM)
    hbm = pl.BlockSpec(memory_space=pl.ANY)
    return pl.pallas_call(
        kernel,
        out_shape=jax.ShapeDtypeStruct((ROWS, COLS), BF16),
        in_specs=[vmem, hbm, hbm, hbm, vmem, vmem],
        out_specs=vmem,
        scratch_shapes=[
            pltpu.VMEM((WIDTH, WIDTH), BF16),
            pltpu.VMEM((128, WIDTH), BF16),
            pltpu.VMEM((128, COLS), BF16),
            pltpu.VMEM((16, 2, ROWS, WPAD), BF16),
            pltpu.VMEM((4, 256, WPAD), BF16),
            pltpu.VMEM((128, WPAD), BF16),
            pltpu.VMEM((CHUNKS, 8, CROWS, 128), F32),
            pltpu.VMEM((CHUNKS, 8, CROWS, 128), F32),
            pltpu.VMEM((CHUNKS, 2, CROWS, 128), BF16),
            pltpu.VMEM((16, 128, 128), BF16),
            pltpu.VMEM((CHUNKS, 8, CROWS, 128), BF16),
            pltpu.VMEM((CHUNKS, 7, CROWS, 128), BF16),
            pltpu.VMEM((CROWS, 128), F32),
            pltpu.VMEM((CHUNKS, 4, SPAD, 128), BF16),
            pltpu.VMEM((NDP, SPAD, 128), BF16),
            pltpu.VMEM((COLS, 128), F32),
            pltpu.VMEM((16, 128, 128), BF16),
            pltpu.VMEM((NZ, 4, 128), F32),
            pltpu.VMEM((NZ, 4, 128), F32),
            pltpu.VMEM((4, 128), F32),
            pltpu.VMEM((NZ, 4, 128), F32),
            pltpu.VMEM((64, 128), F32),
            pltpu.VMEM((128, 128), F32),
            pltpu.VMEM((8, 16, CPAD), BF16),
            pltpu.VMEM((8, 16, CPAD), BF16),
            pltpu.VMEM((4, 32, CPAD), BF16),
            pltpu.VMEM((4, 32, CPAD), BF16),
            pltpu.VMEM((ROWS, COLS), F32),
            dma((3,)), dma((len(PARTS),)), dma((len(PARTS),)), dma((16,)), dma((16,)),
            dma((CHUNKS, 8)), dma((CHUNKS, 8)), dma((CHUNKS, 7)), dma((CHUNKS, 7)),
            dma((CHUNKS, 4, 2)), dma((CHUNKS, 4, 2)),
            dma((NZ,)), dma((NZ,)), dma((NZ,)), dma((NZ,)),
            dma((8,)), dma((8,)), dma((4,)), dma((4,)),
        ],
        compiler_params=pltpu.CompilerParams(
            collective_id=0, has_side_effects=True, vmem_limit_bytes=56 * 1024 * 1024
        ),
        name="gather_sum_exchange",
    )(
        tokens,
        base_up_matrix.reshape(WIDTH, WIDTH),
        adapter_down_maps.reshape(128, WIDTH),
        adapter_up_maps.reshape(128, COLS),
        request_adapter.reshape(1, ROWS),
        adapter_storage.reshape(1, 64),
    )


def solution(mesh):
    return jax.shard_map(
        local,
        mesh=mesh,
        in_specs=(
            P("dp", "tensor"),
            P("tensor", "dp", None),
            P("dp", None, "tensor"),
            P("dp", None, "tensor"),
            P("dp", None),
            P(),
        ),
        out_specs=P("dp", "tensor"),
        check_vma=False,
    )
```

time: 122 us -> 88 us (0.72)
  Pallas kernels: 119 us -> 86.1 us
  local copies, waits for them, and re-layouts: 3.01 us -> 1.66 us
    pallas_call x1, Pallas kernels: 119 us -> 86.1 us  [local(): pl.pallas_call(kernel, out_shape=jax.ShapeDtypeStruct((ROWS, COLS), BF16)...]
    unnamed x2 -> x1, local copies, waits for them, and re-layouts: 3.01 us -> 1.66 us
where the time goes in v2:
time: 88 us; the launch traced here: 87.8 us
  Pallas kernels  86.1 us (98%)
  local copies, waits for them, and re-layouts  1.66 us (2%)
    pallas_call x1, Pallas kernels, local(): pl.pallas_call(kernel, out_shape=jax.ShapeDtypeStruct((ROWS, COLS), BF16)...  86.1 us

profile of v2, /device:TPU:1, one launch (start us, length us, event | category | flops | bytes accessed | tf_op | source)
XLA Modules:
  0.0 87.8 jit_solution(11183140447877432688)
XLA Ops:
  0.0 86.1 %gather_sum_exchange.1 = bf16[64,1856]{1,0:T(8,128)(2,1)} custom-call(bf16[64,928]{1,0:T(8,128)(2,1)} %tok_ref.1, bf16[928,928]{1,0:T(8,128)(2,1)} %bitcast.5, bf16[128,928]{1,0:T(8,128)(2,1)} %bitcast.7, bf16[128,1856]{1,0:T(8,128)(2,1)} %bitcast.6, s32[1,64]{1,0:T(1,128)} %bitcast.8, s32[1,64]{1,0:T(1,128)} %bitcast.9), custom_call_target="tpu_custom_call" | custom-call | tf_op jit(solution)/shard_map/gather_sum_exchange/pallas_call | solution.py:447
  86.2 1.7 %copy.8 = bf16[64,1856]{1,0:T(8,128)(2,1)} copy(bf16[64,1856]{1,0:T(8,128)(2,1)} %gather_sum_exchange.1) | data formatting | bytes 475136

commit v3 on v2

--- a/solution.py
+++ b/solution.py
@@ -82,7 +82,7 @@
 def kernel(
     tok_ref, w_any, down_any, up_any, req_ref, sto_ref, out_ref,
     w_ref, down_ref, up_ref, xbuf, wt, low, ylong, yshort, first, h, lbuf, sbuf, both, total, rbuf, stack, sel,
-    zsend, zrecv, zred, zgather, shr, shrx, dbuf, ebuf, fbuf, gbuf, dterm,
+    zsend, zrecv, zred, zgather, shrx, dbuf, ebuf, fbuf, gbuf, dterm,
     in_s, ag_s, ag_r, fw_s, fw_r, l_s, l_r, s_s, s_r, r_s, r_r,
     z1_s, z1_r, z2_s, z2_r, e_s, e_r, g_s, g_r,
 ):
@@ -91,13 +91,21 @@
     core = lax.rem(dp, 2)
     cy = lax.rem(dp // 2, 4)
     cx = dp // 8
-    yc = cy * 2 + core
+    along_own = cy + core * (cx - cy)
+    first_core = along_own * 2 + core
+    e_slot = core * 4 + along_own
+    z_own = lax.rem(cx + cy + 2 * core, 4)
     way = 1 - 2 * core
 
     def dev(x, yy, c):
         return (lax.rem(x, 4) * 4 + lax.rem(yy, 4)) * 2 + c
 
     partner = dev(cx, cy, 1 - core)
+
+    def along_first(other):
+        spot, c = other // 2, lax.rem(other, 2)
+        return dev(cx + core * (spot + 4 - cx), spot + core * (cy + 4 - spot), c)
+
     steps = {
         ("f", 1): dev(cx + core, cy + 1 - core, core),
         ("f", 3): dev(cx + 3 * core, cy + 3 * (1 - core), core),
@@ -235,12 +243,12 @@
     def result(n, q, c):
         dx, dy = OFFSETS[n][q]
         target = dev(cx + 4 - dx, cy + 4 - dy, c)
-        return remote(total.at[n, q], rbuf.at[dp], r_s.at[n, q, c], r_r.at[n, q, core], (target, z))
+        return remote(total.at[n, q, c], rbuf.at[dp], r_s.at[n, q, c], r_r.at[n, q, core], (target, z))
 
     def result_arrives(n, q, c):
         dx, dy = OFFSETS[n][q]
         source = dev(cx + dx, cy + dy, c)
-        return remote(total.at[n, q], rbuf.at[source], r_s.at[n, q, c], r_r.at[n, q, c], (partner, z))
+        return remote(total.at[n, q, c], rbuf.at[source], r_s.at[n, q, c], r_r.at[n, q, c], (partner, z))
 
     def others(n, q, c, what):
         if n == 0 and q == 0:
@@ -251,6 +259,8 @@
 
         else:
             what(n, q, c)
+
+    left = iota((32, 128), 1) < 64
 
     def stage(n, s):
         if s == 0:
@@ -273,11 +283,14 @@
             long_hop(n, 7, lbuf.at[n, 7]).wait_recv()
             both[...] = lbuf[n, 7].astype(F32) + sbuf[n, 6].astype(F32) + yshort[n, 7]
             for q in range(4):
-                total[n, q] = both[q * SHARE : q * SHARE + SPAD].astype(BF16)
+                upper = both[q * SHARE : q * SHARE + 32]
+                under = both[q * SHARE + 32 : q * SHARE + 64]
+                total[n, q, 0] = jnp.where(left, upper, pltpu.roll(under, 64, 1)).astype(BF16)
+                total[n, q, 1] = jnp.where(left, pltpu.roll(upper, 64, 1), under).astype(BF16)
                 for c in range(2):
                     others(n, q, c, lambda *a: result(*a).start())
             if n == 0:
-                rbuf[dp] = total[0, 0]
+                rbuf[dp] = total[0, 0, core]
 
     lane64 = iota((64, 128), 1)
 
@@ -289,56 +302,60 @@
                 dx, dy = OFFSETS[n][q]
                 x = lax.rem(cx + 4 - dx, 4)
                 yy = lax.rem(cy + 4 - dy, 4)
+                along, across = yy + core * (x - yy), x + core * (yy - x)
                 meta = dot_nt(
                     jnp.where(iota((16, 128), 1) == 127, 1.0, 0.0).astype(BF16),
                     xbuf[p, :, :, WPAD - 128 : WPAD].reshape(128, 128),
                 )[0:1]
                 row = iota((128, 128), 0)
-                home = (yy * 2 + iota((128, 128), 1) // 64) * 4 + x
+                home = (along * 2 + iota((128, 128), 1) // 64) * 4 + across
                 wanted = key + 2 * (row // 64) + row % 2
                 hit = ((row % 64) // 2 == home) & (meta.astype(jnp.int32) == wanted)
                 sel[p] = jnp.where(hit, 1.0, 0.0).astype(BF16)
         acc = jnp.zeros((128, 128), F32)
         for p in range(16):
             acc = acc + dot_nt(sel[p], h[p])
-        part = jnp.where(lane64 < 64, acc[0:64], acc[64:128])
-        for i in range(NZ):
-            zsend[i] = part[4 * i : 4 * i + 4]
-
-        @pl.loop(1, NZ)
-        def _(i):
-            other = lax.rem(z + i, NZ)
-            remote(zsend.at[other], zrecv.at[z], z1_s.at[i], z1_r.at[i], (dp, other)).start()
-
-        zrecv[z] = zsend[z]
+        part = jnp.where(lane64 < 64, acc[0:64], acc[64:128]).astype(BF16)
+        for q in range(4):
+            zsend[q] = part[16 * q : 16 * q + 16]
+            owner = 4 * q + z_own
+
+            @pl.when(owner != z)
+            def _():
+                remote(zsend.at[q], zrecv.at[z], z1_s.at[q], z1_r.at[z], (dp, owner)).start()
+
+            @pl.when(owner == z)
+            def _():
+                zrecv[z] = zsend[q]
 
     def reduce():
-        @pl.loop(1, NZ)
-        def _(i):
-            other = lax.rem(z + NZ - i, NZ)
-            remote(zsend.at[other], zrecv.at[other], z1_s.at[i], z1_r.at[i], (dp, other)).wait_recv()
-
-        whole = zrecv[0]
-        for i in range(1, NZ):
-            whole = whole + zrecv[i]
-        zred[...] = whole
-
-        @pl.loop(1, NZ)
-        def _(i):
-            other = lax.rem(z + i, NZ)
-            remote(zred, zgather.at[z], z2_s.at[i], z2_r.at[i], (dp, other)).start()
-
-        zgather[z] = zred[...]
+        @pl.when(lax.rem(z, 4) == z_own)
+        def _():
+            @pl.loop(1, NZ)
+            def _(i):
+                other = lax.rem(z + i, NZ)
+                remote(zsend.at[0], zrecv.at[other], z1_s.at[0], z1_r.at[other], (dp, other)).wait_recv()
+
+            whole = zrecv[0].astype(F32)
+            for i in range(1, NZ):
+                whole = whole + zrecv[i].astype(F32)
+            zred[...] = whole.astype(BF16)
+
+            @pl.loop(1, NZ)
+            def _(i):
+                other = lax.rem(z + i, NZ)
+                remote(zred, zgather.at[z // 4], z2_s.at[i], z2_r.at[z // 4], (dp, other)).start()
+
+            zgather[z // 4] = zred[...]
 
     def grow():
-        @pl.loop(1, NZ)
-        def _(i):
-            other = lax.rem(z + NZ - i, NZ)
-            remote(zred, zgather.at[other], z2_s.at[i], z2_r.at[i], (dp, other)).wait_recv()
-
-        for i in range(NZ):
-            shr[4 * i : 4 * i + 4] = zgather[i]
-        rows = shr[...]
+        for q in range(4):
+
+            @pl.when(4 * q + z_own != z)
+            def _():
+                remote(zred, zgather.at[q], z2_s.at[1], z2_r.at[q], (dp, 4 * q + z_own)).wait_recv()
+
+        rows = zgather[...].reshape(64, 128).astype(F32)
         for g in range(8):
             eight = rows[8 * g : 8 * g + 8]
             lane = lane64[0:8]
@@ -350,38 +367,44 @@
 
         @pl.loop(1, 8)
         def _(i):
-            other = lax.rem(yc + i, 8)
-            target = dev(cx, other // 2, lax.rem(other, 2))
-            remote(dbuf.at[other], ebuf.at[yc], e_s.at[i], e_r.at[i], (target, z)).start()
-
-        ebuf[yc] = dbuf[yc]
+            other = lax.rem(first_core + i, 8)
+            remote(dbuf.at[other], ebuf.at[e_slot], e_s.at[i], e_r.at[e_slot], (along_first(other), z)).start()
+
+        ebuf[e_slot] = dbuf[first_core]
 
     def sort():
         @pl.loop(1, 8)
         def _(i):
-            other = lax.rem(yc + 8 - i, 8)
-            target = dev(cx, other // 2, lax.rem(other, 2))
-            remote(dbuf.at[other], ebuf.at[other], e_s.at[i], e_r.at[i], (target, z)).wait_recv()
+            slot = lax.rem(e_slot + i, 8)
+            remote(dbuf.at[slot], ebuf.at[slot], e_s.at[i], e_r.at[slot], (partner, z)).wait_recv()
 
         to = iota((128, 128), 0)
-        source = ((to // 4) % 8) * 16 + ((to // 2) % 2) * 8 + (to // 32) * 2 + to % 2
+        place_of = to // 16
+        origin = (place_of // 4) * 4 + (to // 4) % 4
+        source = origin * 16 + ((to // 2) % 2) * 8 + (place_of % 4) * 2 + to % 2
         perm = jnp.where(iota((128, 128), 1) == source, 1.0, 0.0).astype(BF16)
-        fbuf[...] = dot_nn(perm, ebuf[...].reshape(128, CPAD)).reshape(4, 32, CPAD).astype(BF16)
+        fbuf[...] = dot_nn(perm, ebuf[...].reshape(128, CPAD)).reshape(8, 16, CPAD).astype(BF16)
 
         @pl.loop(1, 4)
         def _(i):
-            other = lax.rem(cx + i, 4)
-            remote(fbuf.at[other], gbuf.at[cx], g_s.at[i], g_r.at[i], (dev(other, cy, core), z)).start()
+            to_x, to_y = lax.rem(cx + i, 4), lax.rem(cy + i, 4)
+            remote(fbuf.at[to_x], gbuf.at[cx], g_s.at[i], g_r.at[i], (dev(to_x, cy, core), z)).start()
+            remote(fbuf.at[4 + to_y], gbuf.at[4 + cy], g_s.at[4 + i], g_r.at[4 + i], (dev(cx, to_y, core), z)).start()
 
         gbuf[cx] = fbuf[cx]
+        gbuf[4 + cy] = fbuf[4 + cy]
 
     def deltas():
         @pl.loop(1, 4)
         def _(i):
-            other = lax.rem(cx + 4 - i, 4)
-            remote(fbuf.at[other], gbuf.at[other], g_s.at[i], g_r.at[i], (dev(other, cy, core), z)).wait_recv()
-
-        mine = (place.astype(jnp.int32) == iota((ROWS, 128), 1)).astype(F32).astype(BF16)
+            of_x, of_y = lax.rem(cx + 4 - i, 4), lax.rem(cy + 4 - i, 4)
+            remote(fbuf.at[0], gbuf.at[of_x], g_s.at[i], g_r.at[i], (partner, z)).wait_recv()
+            remote(fbuf.at[0], gbuf.at[4 + of_y], g_s.at[4 + i], g_r.at[4 + i], (partner, z)).wait_recv()
+
+        lane = iota((ROWS, 128), 1)
+        line, step = lane // 16, (lane // 4) % 4
+        owner = jnp.where(line < 4, (line * 4 + step) * 2, (step * 4 + line - 4) * 2 + 1)
+        mine = (place.astype(jnp.int32) == owner * 4 + lane % 4).astype(F32).astype(BF16)
         dterm[...] = dot_nn(mine, gbuf[...].reshape(128, CPAD))[:, 0:COLS]
 
     adapters = {"shrink": shrink, "reduce": reduce, "grow": grow, "sort": sort, "delta": deltas}
@@ -410,19 +433,26 @@
         for s in range(7):
             short_hop(n, s, sbuf.at[n, s]).wait_send()
 
-    @pl.loop(1, NZ)
-    def _(i):
-        other = lax.rem(z + i, NZ)
-        remote(zsend.at[other], zrecv.at[z], z1_s.at[i], z1_r.at[i], (dp, other)).wait_send()
-        remote(zred, zgather.at[z], z2_s.at[i], z2_r.at[i], (dp, other)).wait_send()
+    for q in range(4):
+
+        @pl.when(4 * q + z_own != z)
+        def _():
+            remote(zsend.at[q], zrecv.at[z], z1_s.at[q], z1_r.at[z], (partner, z)).wait_send()
+
+    @pl.when(lax.rem(z, 4) == z_own)
+    def _():
+        @pl.loop(1, NZ)
+        def _(i):
+            remote(zred, zgather.at[0], z2_s.at[i], z2_r.at[0], (partner, z)).wait_send()
 
     @pl.loop(1, 8)
     def _(i):
-        remote(dbuf.at[yc], ebuf.at[yc], e_s.at[i], e_r.at[i], (partner, z)).wait_send()
+        remote(dbuf.at[i], ebuf.at[i], e_s.at[i], e_r.at[i], (partner, z)).wait_send()
 
     @pl.loop(1, 4)
     def _(i):
-        remote(fbuf.at[cx], gbuf.at[cx], g_s.at[i], g_r.at[i], (partner, z)).wait_send()
+        remote(fbuf.at[0], gbuf.at[0], g_s.at[i], g_r.at[i], (partner, z)).wait_send()
+        remote(fbuf.at[0], gbuf.at[0], g_s.at[4 + i], g_r.at[4 + i], (partner, z)).wait_send()
 
     for n in range(CHUNKS):
         for q in range(4):
@@ -434,8 +464,10 @@
                 others(n, q, c, lambda *a: result_arrives(*a).wait_recv())
 
     for k in range(NDP):
-        stack[k * SHARE : (k + 1) * SHARE] = rbuf[k].astype(F32)[0:SHARE]
-    turn = jnp.where(iota((ROWS, 128), 1) == core * 64 + iota((ROWS, 128), 0), 1.0, 0.0).astype(BF16)
+        got = rbuf[k].astype(F32)
+        stack[k * SHARE : k * SHARE + 32] = jnp.where(left, got, 0.0)
+        stack[k * SHARE + 32 : (k + 1) * SHARE] = jnp.where(left, 0.0, got)[0 : SHARE - 32]
+    turn = jnp.where(iota((ROWS, 128), 1) % 64 == iota((ROWS, 128), 0), 1.0, 0.0).astype(BF16)
     v = dot_nt(turn, stack[...].astype(BF16)) + dterm[...]
     out_ref[...] = (0.5 * v * (1.0 + erf(v * 0.7071067811865476))).astype(BF16)
 
@@ -463,26 +495,25 @@
             pltpu.VMEM((CHUNKS, 8, CROWS, 128), BF16),
             pltpu.VMEM((CHUNKS, 7, CROWS, 128), BF16),
             pltpu.VMEM((CROWS, 128), F32),
-            pltpu.VMEM((CHUNKS, 4, SPAD, 128), BF16),
-            pltpu.VMEM((NDP, SPAD, 128), BF16),
+            pltpu.VMEM((CHUNKS, 4, 2, 32, 128), BF16),
+            pltpu.VMEM((NDP, 32, 128), BF16),
             pltpu.VMEM((COLS, 128), F32),
             pltpu.VMEM((16, 128, 128), BF16),
-            pltpu.VMEM((NZ, 4, 128), F32),
-            pltpu.VMEM((NZ, 4, 128), F32),
-            pltpu.VMEM((4, 128), F32),
-            pltpu.VMEM((NZ, 4, 128), F32),
-            pltpu.VMEM((64, 128), F32),
+            pltpu.VMEM((4, 16, 128), BF16),
+            pltpu.VMEM((NZ, 16, 128), BF16),
+            pltpu.VMEM((16, 128), BF16),
+            pltpu.VMEM((4, 16, 128), BF16),
             pltpu.VMEM((128, 128), F32),
             pltpu.VMEM((8, 16, CPAD), BF16),
             pltpu.VMEM((8, 16, CPAD), BF16),
-            pltpu.VMEM((4, 32, CPAD), BF16),
-            pltpu.VMEM((4, 32, CPAD), BF16),
+            pltpu.VMEM((8, 16, CPAD), BF16),
+            pltpu.VMEM((8, 16, CPAD), BF16),
             pltpu.VMEM((ROWS, COLS), F32),
             dma((3,)), dma((len(PARTS),)), dma((len(PARTS),)), dma((16,)), dma((16,)),
             dma((CHUNKS, 8)), dma((CHUNKS, 8)), dma((CHUNKS, 7)), dma((CHUNKS, 7)),
             dma((CHUNKS, 4, 2)), dma((CHUNKS, 4, 2)),
-            dma((NZ,)), dma((NZ,)), dma((NZ,)), dma((NZ,)),
-            dma((8,)), dma((8,)), dma((4,)), dma((4,)),
+            dma((4,)), dma((NZ,)), dma((NZ,)), dma((4,)),
+            dma((8,)), dma((8,)), dma((8,)), dma((8,)),
         ],
         compiler_params=pltpu.CompilerParams(
             collective_id=0, has_side_effects=True, vmem_limit_bytes=56 * 1024 * 1024

time: 88 us -> 84.2 us (0.957)
  Pallas kernels: 86.1 us -> 82.4 us
    pallas_call x1, Pallas kernels: 86.1 us -> 82.4 us  [local(): pl.pallas_call(kernel, out_shape=jax.ShapeDtypeStruct((ROWS, COLS), BF16)...]
where the time goes in v3:
time: 84.2 us; the launch traced here: 84.1 us
  Pallas kernels  82.4 us (98%)
  local copies, waits for them, and re-layouts  1.66 us (2%)
    pallas_call x1, Pallas kernels, local(): pl.pallas_call(kernel, out_shape=jax.ShapeDtypeStruct((ROWS, COLS), BF16)...  82.4 us

profile of v3, /device:TPU:1, one launch (start us, length us, event | category | flops | bytes accessed | tf_op | source)
XLA Modules:
  0.0 84.1 jit_solution(17961009710605206947)
XLA Ops:
  0.0 82.4 %gather_sum_exchange.1 = bf16[64,1856]{1,0:T(8,128)(2,1)} custom-call(bf16[64,928]{1,0:T(8,128)(2,1)} %tok_ref.1, bf16[928,928]{1,0:T(8,128)(2,1)} %bitcast.5, bf16[128,928]{1,0:T(8,128)(2,1)} %bitcast.7, bf16[128,1856]{1,0:T(8,128)(2,1)} %bitcast.6, s32[1,64]{1,0:T(1,128)} %bitcast.8, s32[1,64]{1,0:T(1,128)} %bitcast.9), custom_call_target="tpu_custom_call" | custom-call | tf_op jit(solution)/shard_map/gather_sum_exchange/pallas_call | solution.py:479
  82.4 1.7 %copy.8 = bf16[64,1856]{1,0:T(8,128)(2,1)} copy(bf16[64,1856]{1,0:T(8,128)(2,1)} %gather_sum_exchange.1) | data formatting | bytes 475136

commit v4 on v3

--- a/solution.py
+++ b/solution.py
@@ -37,14 +37,15 @@
 
 ORDER = (
     "w0", "w1", "w2", "w3", "10F", "30F", "01F", "03F", "20a", "m00",
-    "13F", "s00", "11F", "20b", "m01", "m02", "m03", "31F", "33F", "02a",
-    "02b", "l0", "s01", "12b", "12a", "m10", "s10", "m11", "21F", "23F",
-    "m12", "32a", "32b", "m13", "s02", "m20", "s20", "22a", "22b", "s11",
-    "m21", "m22", "m23", "m30", "s30", "s03", "m31", "m32", "s21", "m33",
-    "l1", "s12", "l2", "l3", "shrink", "s31", "s22", "s13", "s32", "s23",
-    "s14", "reduce", "s33", "s24", "s04", "s34", "s25", "s15", "grow", "s35",
-    "s05", "s26", "s36", "s16", "s06", "sort", "s37", "s27", "s17", "s07",
-    "s38", "s28", "delta", "s18", "s08",
+    "13F", "r1", "s00", "11F", "20b", "m01", "m02", "m03", "r2", "31F",
+    "33F", "02a", "02b", "l0", "s01", "r3", "12b", "12a", "m10", "s10",
+    "m11", "21F", "r4", "23F", "m12", "32a", "32b", "m13", "s02", "m20",
+    "r5", "s20", "22a", "22b", "s11", "m21", "m22", "r6", "m23", "m30",
+    "s30", "s03", "m31", "m32", "r7", "s21", "m33", "l1", "s12", "l2",
+    "l3", "r8", "shrink", "s31", "s22", "s13", "s32", "s23", "s14", "reduce",
+    "s33", "s24", "s04", "s34", "s25", "s15", "grow", "s35", "s05", "s26",
+    "s36", "s16", "s06", "sort", "s37", "s27", "s17", "s07", "s38", "s28",
+    "delta", "s18", "s08",
 )
 
 
@@ -84,7 +85,7 @@
     w_ref, down_ref, up_ref, xbuf, wt, low, ylong, yshort, first, h, lbuf, sbuf, both, total, rbuf, stack, sel,
     zsend, zrecv, zred, zgather, shrx, dbuf, ebuf, fbuf, gbuf, dterm,
     in_s, ag_s, ag_r, fw_s, fw_r, l_s, l_r, s_s, s_r, r_s, r_r,
-    z1_s, z1_r, z2_s, z2_r, e_s, e_r, g_s, g_r,
+    z1_s, z1_r, z2_s, z2_r, e_s, e_r, g_s, g_r, ring,
 ):
     dp = lax.axis_index("dp")
     z = lax.axis_index("tensor")
@@ -119,14 +120,11 @@
         )
 
     barrier = pltpu.get_barrier_semaphore()
-
-    @pl.loop(1, NZ)
-    def _(i):
-        pl.semaphore_signal(barrier, inc=1, device_id=(dp, lax.rem(z + i, NZ)), device_id_type=MESH)
-
-    @pl.loop(1, NDP)
-    def _(i):
-        pl.semaphore_signal(barrier, inc=1, device_id=(lax.rem(dp + i, NDP), z), device_id_type=MESH)
+    above, below = (dp, lax.rem(z + 1, NZ)), (dp, lax.rem(z + NZ - 1, NZ))
+    near = [(dev(cx + 1, cy, core), z), (dev(cx + 3, cy, core), z), (dev(cx, cy + 1, core), z)]
+    near += [(dev(cx, cy + 3, core), z), (partner, z), above, below]
+    for device in near:
+        pl.semaphore_signal(barrier, inc=1, device_id=device, device_id_type=MESH)
 
     loads = {
         "w": pltpu.make_async_copy(w_any, w_ref, in_s.at[0]),
@@ -147,7 +145,17 @@
     xbuf[0, core, :, WPAD - 128 : WPAD] = jnp.broadcast_to(place, (ROWS, 128)).astype(BF16)
     xbuf[0, core, :, 0:WIDTH] = tok_ref[...]
 
-    pl.semaphore_wait(barrier, NDP - 1 + NZ - 1)
+    pl.semaphore_wait(barrier, len(near))
+
+    def greet(k):
+        if k > 0:
+            pl.semaphore_wait(ring.at[0], 1)
+            pl.semaphore_wait(ring.at[1], 1)
+        if k < 8:
+            pl.semaphore_signal(ring.at[0], inc=1, device_id=above, device_id_type=MESH)
+            pl.semaphore_signal(ring.at[1], inc=1, device_id=below, device_id_type=MESH)
+
+    greet(0)
 
     def where_at(f, g):
         return POS[g, f] + core * (POS[f, g] - POS[g, f])
@@ -411,6 +419,8 @@
     for word in ORDER:
         if word in adapters:
             adapters[word]()
+        elif word[0] == "r":
+            greet(int(word[1]))
         elif word[0] == "w":
             weights(int(word[1]))
         elif word[0] == "m":
@@ -514,6 +524,7 @@
             dma((CHUNKS, 4, 2)), dma((CHUNKS, 4, 2)),
             dma((4,)), dma((NZ,)), dma((NZ,)), dma((4,)),
             dma((8,)), dma((8,)), dma((8,)), dma((8,)),
+            pltpu.SemaphoreType.REGULAR((2,)),
         ],
         compiler_params=pltpu.CompilerParams(
             collective_id=0, has_side_effects=True, vmem_limit_bytes=56 * 1024 * 1024

time: 84.2 us -> 81.5 us (0.968)
  Pallas kernels: 82.4 us -> 79.7 us
    pallas_call x1, Pallas kernels: 82.4 us -> 79.7 us  [local(): pl.pallas_call(kernel, out_shape=jax.ShapeDtypeStruct((ROWS, COLS), BF16)...]
where the time goes in v4:
time: 81.5 us; the launch traced here: 81.3 us
  Pallas kernels  79.7 us (98%)
  local copies, waits for them, and re-layouts  1.66 us (2%)
    pallas_call x1, Pallas kernels, local(): pl.pallas_call(kernel, out_shape=jax.ShapeDtypeStruct((ROWS, COLS), BF16)...  79.7 us
    unnamed x1, local copies, waits for them, and re-layouts  1.66 us

profile of v4, /device:TPU:1, one launch (start us, length us, event | category | flops | bytes accessed | tf_op | source)
XLA Modules:
  0.0 81.3 jit_solution(6533167620677772536)
XLA Ops:
  0.0 79.7 %gather_sum_exchange.1 = bf16[64,1856]{1,0:T(8,128)(2,1)} custom-call(bf16[64,928]{1,0:T(8,128)(2,1)} %tok_ref.1, bf16[928,928]{1,0:T(8,128)(2,1)} %bitcast.5, bf16[128,928]{1,0:T(8,128)(2,1)} %bitcast.7, bf16[128,1856]{1,0:T(8,128)(2,1)} %bitcast.6, s32[1,64]{1,0:T(1,128)} %bitcast.8, s32[1,64]{1,0:T(1,128)} %bitcast.9), custom_call_target="tpu_custom_call" | custom-call | tf_op jit(solution)/shard_map/gather_sum_exchange/pallas_call | solution.py:489
  79.7 1.7 %copy.8 = bf16[64,1856]{1,0:T(8,128)(2,1)} copy(bf16[64,1856]{1,0:T(8,128)(2,1)} %gather_sum_exchange.1) | data formatting | bytes 475136

commit v5 on v4

--- a/solution.py
+++ b/solution.py
@@ -45,7 +45,7 @@
     "l3", "r8", "shrink", "s31", "s22", "s13", "s32", "s23", "s14", "reduce",
     "s33", "s24", "s04", "s34", "s25", "s15", "grow", "s35", "s05", "s26",
     "s36", "s16", "s06", "sort", "s37", "s27", "s17", "s07", "s38", "s28",
-    "delta", "s18", "s08",
+    "s18", "s08", "delta",
 )
 
 

time: 81.5 us -> 81.5 us (level)
  no operation moved by 1% of the time
where the time goes in v5:
time: 81.5 us; the launch traced here: 81.3 us
  Pallas kernels  79.7 us (98%)
  local copies, waits for them, and re-layouts  1.66 us (2%)
    pallas_call x1, Pallas kernels, local(): pl.pallas_call(kernel, out_shape=jax.ShapeDtypeStruct((ROWS, COLS), BF16)...  79.7 us
    unnamed x1, local copies, waits for them, and re-layouts  1.66 us

profile of v5, /device:TPU:1, one launch (start us, length us, event | category | flops | bytes accessed | tf_op | source)
XLA Modules:
  0.0 81.3 jit_solution(10629528327329986742)
XLA Ops:
  0.0 79.7 %gather_sum_exchange.1 = bf16[64,1856]{1,0:T(8,128)(2,1)} custom-call(bf16[64,928]{1,0:T(8,128)(2,1)} %tok_ref.1, bf16[928,928]{1,0:T(8,128)(2,1)} %bitcast.5, bf16[128,928]{1,0:T(8,128)(2,1)} %bitcast.7, bf16[128,1856]{1,0:T(8,128)(2,1)} %bitcast.6, s32[1,64]{1,0:T(1,128)} %bitcast.8, s32[1,64]{1,0:T(1,128)} %bitcast.9), custom_call_target="tpu_custom_call" | custom-call | tf_op jit(solution)/shard_map/gather_sum_exchange/pallas_call | solution.py:489
  79.7 1.7 %copy.8 = bf16[64,1856]{1,0:T(8,128)(2,1)} copy(bf16[64,1856]{1,0:T(8,128)(2,1)} %gather_sum_exchange.1) | data formatting | bytes 475136
